TPU v7x, 32 devices: a whole 2x2x4 slice. The times are simulated.
32 devices in a mesh: pair: 4 (over y, x), col: 8 (over z, core).
Axes of the slice: x: 2, y: 2, z: 4, core: 2. Of those that a mesh axis runs over, the one named last changes fastest.
Arguments:
- amplitudes: float32 [2048, 2048], P('pair', 'col'), may hold values from -6 to 6
- integrals: float32 [2048, 2048], P('pair', 'col'), may hold values from -0.25 to 0.25
- amp_tiles: int32 [4, 8, 4], P('pair', 'col'), may hold values from 0 to 7, as said below
- amp_count: int32 [4, 8], P('pair', 'col'), may hold values from 1 to 4, as said below
- int_mask: int32 [16, 16], P('pair', 'col'), may hold values 0 or 1
Outputs:
- ladder: float32 [2048, 2048], P('pair', 'col')
Inputs may be any that keep to these rules, and one draw needn't show every extreme that they name: `amp_tiles`: in each device's list the entries are distinct tile numbers of that device's block. `amp_count`: some device's count equals 4 in every draw.
All inputs are finite; a program needn't handle non-finite values. No bound on the sum of `int_mask` on one device may be relied on, other than what follows from the above.
Results may differ from a plain program's by a relative error of at most 0.00007.
Values sent between devices are 32-bit elements; how exact they have to be, the bound alone decides.
A program may use at most 128 MiB of HBM per device.

v0:
```python
import jax
import jax.numpy as jnp
from jax import lax
from jax.sharding import PartitionSpec as P

TILE = 128


def expand_tiles(tile_mask):
    row_tiles = tile_mask.shape[0]
    col_tiles = tile_mask.shape[1]
    widened = jnp.broadcast_to(tile_mask[:, None, :, None], (row_tiles, TILE, col_tiles, TILE))
    return widened.reshape(row_tiles * TILE, col_tiles * TILE)


def local(amplitudes, integrals, amp_tiles, amp_count, int_mask):
    tile_rows = amplitudes.shape[0] // TILE
    tile_cols = amplitudes.shape[1] // TILE
    tile_list = amp_tiles[0, 0]
    slot_index = jnp.arange(tile_list.shape[0], dtype=jnp.int32)
    is_live = slot_index < amp_count[0, 0]
    own_tiles = amplitudes.reshape(tile_rows, TILE, tile_cols, TILE).transpose(0, 2, 1, 3)
    own_tiles = own_tiles.reshape(tile_rows * tile_cols, TILE, TILE)
    packed = own_tiles[tile_list] * is_live.astype(jnp.float32)[:, None, None]
    received, received_ids = (
        lax.all_gather(packed, "col", axis=0, tiled=True),
        lax.all_gather(tile_list, "col", axis=0, tiled=True),
    )
    col_count = lax.axis_size("col")
    source_col = jnp.arange(received_ids.shape[0], dtype=jnp.int32) // tile_list.shape[0]
    dense_index = (
        received_ids // tile_cols * (col_count * tile_cols)
        + source_col * tile_cols
        + received_ids % tile_cols
    )
    dense_tiles = (
        jnp.zeros((tile_rows * col_count * tile_cols, TILE, TILE), jnp.float32)
        .at[dense_index]
        .add(received)
    )
    dense_tiles = dense_tiles.reshape(tile_rows, col_count * tile_cols, TILE, TILE).transpose(
        0, 2, 1, 3
    )
    panel_whole = dense_tiles.reshape(tile_rows * TILE, col_count * tile_cols * TILE)
    int_sparse = integrals * expand_tiles(int_mask.astype(jnp.float32))
    return jnp.dot(
        panel_whole,
        lax.all_gather(int_sparse, "pair", axis=0, tiled=True),
        precision=lax.Precision.HIGHEST,
        preferred_element_type=jnp.float32,
    )


def solution(mesh):
    return jax.shard_map(
        local,
        mesh=mesh,
        in_specs=(
            P("pair", "col"),
            P("pair", "col"),
            P("pair", "col", None),
            P("pair", "col"),
            P("pair", "col"),
        ),
        out_specs=P("pair", "col"),
        check_vma=False,
    )
```

profile of v0, /device:TPU:0, one launch (start us, length us, event | category | flops | bytes accessed | tf_op | source)
XLA Modules:
  0.0 94.1 jit_solution(4700190638760176529)
XLA Ops:
  6.5 0.0 copy-start.3
  6.5 0.0 copy-start.2
  6.5 0.0 copy-start.1
  6.5 0.0 all-gather.4.cloned.1.call-start
  6.5 1.4 %reshape.49 = f32[4,128,2,128]{3,2,1,0:T(2,128)S(1)} reshape(f32[512,256]{1,0:T(8,128)} %param.5) | data formatting | bytes 1048576 | tf_op jit(solution)/shard_map/reshape | solution.py:22
  7.9 0.7 fusion.6
  9.3 0.6 gather_fusion
  9.9 0.8 broadcast_multiply_fusion
  10.6 0.0 all-gather.4.cloned.1.call-update
  10.7 0.0 all-gather.6.cloned.1.call-start
  10.7 0.7 convert_element_type.11
  11.4 0.1 copy.13
  11.5 0.2 broadcast_in_dim.16
  11.7 0.0 copy-done.1
  11.7 0.9 bitcast_multiply_fusion
  12.6 0.0 all-gather.6.cloned.1.call-update
  12.6 0.0 copy-done.3
  12.6 0.6 dynamic-slice
  13.9 0.0 copy-done.2
  13.9 0.1 bitcast_dynamic-update-slice_fusion
  14.0 10.7 %all-reduce = s32[32]{0:T(128)S(1)} all-reduce(s32[32]{0:T(128)S(1)} %bitcast_dynamic-update-slice_fusion), channel_id=2, replica_groups=mesh['pair'=4,'col'=8] {'col'}, use_global_device_ids=true, to_apply=%add | all-reduce | flops 32 | bytes 256 | tf_op jit(solution)/shard_map/all_gather | solution.py:27
  24.7 18.0 %all-gather.4.cloned.1.call-done = f32[32,128,128]{2,1,0:T(8,128)} async-done(((f32[4,128,128]{2,1,0:T(8,128)}), f32[32,128,128]{2,1,0:T(8,128)}) %all-gather.4.cloned.1.call-update) | async-done | bytes 2097168 | tf_op jit(solution)/shard_map/all_gather | solution.py:26
  42.7 0.0 copy-start
  42.7 2.5 %broadcast_in_dim.6 = f32[64,128,128]{2,1,0:T(8,128)} broadcast(f32[]{:T(128)} %constant.40.clone.1), dimensions={} | broadcast | bytes 4194308 | tf_op jit(solution)/shard_map/broadcast_in_dim | solution.py:37
  45.2 0.0 copy-done
  45.2 6.3 %scatter_fusion = f32[64,128,128]{2,1,0:T(8,128)} fusion(f32[64,128,128]{2,1,0:T(8,128)} %broadcast_in_dim.6, s32[32]{0:T(128)S(1)} %compare_select_fusion.1, f32[32,128,128]{2,1,0:T(8,128)S(1)} %copy-done), kind=kCustom, calls=%fused_computation.1 | custom fusion | flops 524288 | bytes 6291584 | tf_op jit(solution)/shard_map/scatter-add | solution.py:39
  51.4 6.8 %copy.12 = f32[4,128,16,128]{3,2,1,0:T(8,128)} copy(f32[4,128,16,128]{3,1,2,0:T(8,128)} %bitcast.24) | data formatting | bytes 8388608 | tf_op jit(solution)/shard_map/transpose | solution.py:41
  58.2 21.1 %all-gather.6.cloned.1.call-done = f32[2048,256]{1,0:T(8,128)} async-done(((f32[512,256]{1,0:T(8,128)}), f32[2048,256]{1,0:T(8,128)}) %all-gather.6.cloned.1.call-update) | async-done | bytes 2097168 | tf_op jit(solution)/shard_map/all_gather | solution.py:48
  79.3 7.9 %fusion = f32[512,256]{1,0:T(8,128)} fusion(f32[2048,256]{1,0:T(8,128)} %all-gather.6.cloned.1.call-done, f32[64,8,16,128]{3,2,1,0:T(8,128)} %bitcast.25), kind=kOutput, calls=%fused_computation.2 | convolution fusion | flops 3221225472 | bytes 6815744 | tf_op jit(solution)/shard_map/dot_general | solution.py:46
  (5 shorter events, 0.1 us)
Async XLA Ops:
  6.5 6.1 %copy-start.3 = (u32[32]{0:T(128)S(1)}, u32[32]{0:T(128)}, u32[]{:S(2)}) copy-start(u32[32]{0:T(128)} %constant.54) | copy-start | bytes 388
  6.5 7.3 %copy-start.2 = (s32[1,1,4]{2,1,0:T(1,128)S(1)}, s32[1,1,4]{2,1,0:T(1,128)}, u32[]{:S(2)}) copy-start(s32[1,1,4]{2,1,0:T(1,128)} %param.7) | copy-start | bytes 52
  6.5 5.2 %copy-start.1 = (f32[512,256]{1,0:T(8,128)S(1)}, f32[512,256]{1,0:T(8,128)}, u32[]{:S(2)}) copy-start(f32[512,256]{1,0:T(8,128)} %param.6) | copy-start | bytes 1572868
  6.5 36.2 %all-gather.4.cloned.1.call-start = ((), (), s32[]{:S(2)}) async-start(), calls=%async_computation | async-start | bytes 2359296 | tf_op jit(solution)/shard_map/all_gather | solution.py:26
  10.7 68.6 %all-gather.6.cloned.1.call-start = ((), (), s32[]{:S(2)}) async-start(), calls=%async_computation.1 | async-start | bytes 2621440 | tf_op jit(solution)/shard_map/all_gather | solution.py:48
  42.7 2.5 %copy-start = (f32[32,128,128]{2,1,0:T(8,128)S(1)}, f32[32,128,128]{2,1,0:T(8,128)}, u32[]{:S(2)}) copy-start(f32[32,128,128]{2,1,0:T(8,128)} %all-gather.4.cloned.1.call-done) | copy-start | bytes 6291460
Sparse Core Ops, SparseCore 0:
  10.8 31.8 all-gather.3
  44.6 34.7 all-gather.5
where the time goes:
time: 94.4 us; the launch traced here: 94.1 us
  waiting for transfers between devices  39.1 us (41%)
  between operations  14.8 us (16%)
  local copies, waits for them, and re-layouts  12.2 us (13%)
  blocking collectives  10.7 us (11%)
  other arithmetic  9.29 us (10%)
  matrix products  7.93 us (8%)
    all_gather x1, waiting for transfers between devices, local(): lax.all_gather(int_sparse, 'pair', axis=0, tiled=True)  21.1 us
    all_gather x1, waiting for transfers between devices, local(): lax.all_gather(packed, 'col', axis=0, tiled=True)  18 us
    all_gather x1, blocking collectives, local(): lax.all_gather(tile_list, 'col', axis=0, tiled=True)  10.7 us
    dot_general x1, matrix products, local(): jnp.dot(panel_whole, lax.all_gather(int_sparse, 'pair', axis=0, tiled=Tru...  7.93 us
    transpose x1, local copies, waits for them, and re-layouts, local(): dense_tiles.reshape(tile_rows, col_count * tile_cols, TILE, TILE)  6.75 us
    scatter-add x1, other arithmetic, local(): dense_tiles = jnp.zeros((tile_rows * col_count * tile_cols, TILE, TILE),...  6.26 us
    broadcast_in_dim x1, local copies, waits for them, and re-layouts, local(): jnp.zeros((tile_rows * col_count * tile_cols, TILE, TILE), jnp.float32)  2.45 us
  transfers between devices with their start and end apart: 2, of which 2 were waited for; matrix products, arithmetic and copies ran while one was open for 19% of the time, Pallas kernels for 0%

commit v1 on v0

v1 whole, which is shorter than its diff:
```python
import functools

import jax
import jax.numpy as jnp
from jax import lax
from jax.experimental import pallas as pl
from jax.experimental.pallas import tpu as pltpu
from jax.sharding import PartitionSpec as P

TILE = 128
CORES = 2
MESH = pl.DeviceIdType.MESH
BF16 = jnp.bfloat16
F32 = jnp.float32


def split(value):
    high = value.astype(BF16)
    return high, (value - high.astype(F32)).astype(BF16)


def when(*conditions):
    together = conditions[0]
    for condition in conditions[1:]:
        together = jnp.logical_and(together, condition)
    return pl.when(together)


def kernel(
    n_pair, n_col, list_ref, count_ref, mask_ref, amp_hbm, int_hbm, out_ref,
    amp, packed, slots, ints, a_high, a_low, b_high, b_low,
    load_amp, load_int, amp_recv, amp_send, slot_recv, slot_send, int_recv, int_send,
):
    live = packed.shape[1]
    rows, depth = amp.shape
    tile_cols = depth // TILE
    tiles = (rows // TILE) * tile_cols
    int_rows, int_cols = ints.shape[1:]
    half = int_rows // 2
    piece = TILE
    pieces = half // piece

    pair, col = lax.axis_index("pair"), lax.axis_index("col")
    line, line_at, core = n_col // CORES, col // CORES, col % CORES
    wide = n_pair // 2
    high_at, low_at = pair // wide, pair % wide

    sibling = {"col": line_at * CORES + 1 - core}
    above, below = {"col": col + CORES}, {"col": col - CORES}
    across = {"pair": (1 - high_at) * wide + low_at}
    right, left = {"pair": pair + 1}, {"pair": pair - 1}
    has_above, has_below = line_at < line - 1, line_at > 0
    has_right, has_left = low_at < wide - 1, low_at > 0

    int_loads = [
        pltpu.make_async_copy(
            int_hbm.at[pl.ds(at * piece, piece)],
            ints.at[pair, pl.ds(at * piece, piece)],
            load_int.at[at],
        )
        for at in range(2 * pieces)
    ]
    amp_load = pltpu.make_async_copy(amp_hbm, amp, load_amp)
    amp_load.start()
    for load in int_loads:
        load.start()

    barrier = pltpu.get_barrier_semaphore()
    partners = (
        (sibling, None), (across, None), (above, has_above), (below, has_below),
        (right, has_right), (left, has_left),
    )
    for partner, exists in partners:
        def greet(partner=partner):
            pl.semaphore_signal(barrier, inc=1, device_id=partner, device_id_type=MESH)
        if exists is None:
            greet()
        else:
            pl.when(exists)(greet)
    peers = 2
    for _, exists in partners[2:]:
        peers += jnp.where(exists, 1, 0)
    pl.semaphore_wait(barrier, peers)

    def amp_copy(source, slot, way, target):
        ref = packed.at[source, slot]
        return pltpu.make_async_remote_copy(
            src_ref=ref, dst_ref=ref,
            send_sem=amp_send.at[way, source, slot], recv_sem=amp_recv.at[source, slot],
            device_id=target, device_id_type=MESH,
        )

    def slot_copy(source, way, target):
        ref = slots.at[source]
        return pltpu.make_async_remote_copy(
            src_ref=ref, dst_ref=ref,
            send_sem=slot_send.at[way, source], recv_sem=slot_recv.at[source],
            device_id=target, device_id_type=MESH,
        )

    def int_copy(source, at, way, target):
        ref = ints.at[source, pl.ds(at * piece, piece)]
        return pltpu.make_async_remote_copy(
            src_ref=ref, dst_ref=ref,
            send_sem=int_send.at[way, source, at], recv_sem=int_recv.at[source, at],
            device_id=target, device_id_type=MESH,
        )

    amp_load.wait()
    numbers = [
        jnp.where(
            jnp.full((1, TILE), count_ref[0], jnp.int32) > s,
            jnp.full((1, TILE), list_ref[s], jnp.int32),
            -1,
        )
        for s in range(live)
    ]
    for t in range(tiles):
        place = jnp.full((1, TILE), -1, jnp.int32)
        for s in range(live):
            place = jnp.where(numbers[s] == t, s, place)
        slots[col, pl.ds(t, 1), :] = place

    def send_own_amp(copy):
        pl.when(has_above)(lambda: copy(0, above).start())
        pl.when(has_below)(lambda: copy(1, below).start())
        copy(2, sibling).start()

    send_own_amp(lambda way, target: slot_copy(col, way, target))
    for s in range(live):
        number = jnp.broadcast_to(numbers[s], (TILE, TILE))
        value = jnp.zeros((TILE, TILE), F32)
        for t in range(tiles):
            at = (pl.ds(t // tile_cols * TILE, TILE), pl.ds(t % tile_cols * TILE, TILE))
            value = jnp.where(number == t, amp[at], value)
        packed[col, s] = value
        send_own_amp(lambda way, target, s=s: amp_copy(col, s, way, target))

    def ready(at):
        int_loads[at].wait()
        span = pl.ds(at * piece, piece)
        for c in range(int_cols // TILE):
            keep = mask_ref[at * piece // TILE, c].astype(F32)
            cols = pl.ds(c * TILE, TILE)
            ints[pair, span, cols] = ints[pair, span, cols] * keep

    def send_row(source, at):
        pl.when(has_right)(lambda: int_copy(source, at, 0, right).start())
        pl.when(has_left)(lambda: int_copy(source, at, 1, left).start())

    for u in range(pieces):
        ready(u)
        send_row(pair, u)
        ready(pieces + u)
        int_copy(pair, pieces + u, 2, across).start()
    for u in range(pieces):
        send_row(pair, pieces + u)
        int_copy(pair, u, 2, across).start()

    out_ref[...] = jnp.zeros_like(out_ref)

    def amp_slot(source):
        return jnp.abs(source // CORES - line_at)

    def int_slot(source, part):
        away = jnp.abs(source % wide - low_at)
        same = source // wide == high_at
        near = jnp.where(part == 0, away, jnp.where(away > 0, away + 1, 0))
        far = jnp.where(part == 0, away + 2, jnp.where(away > 0, away + 2, 1))
        return jnp.where(same, near, far)

    def step(now, _):
        def pass_amp(source, exists, way, target, more):
            @when(now >= 1, exists)
            def _():
                slot_copy(source, way, target).wait_recv()
                pl.when(more)(lambda: slot_copy(source, way, target).start())
                slot_copy(source, 2, sibling).start()

        def pass_tile(source, s, exists, way, target, more):
            @when(now >= 1, exists)
            def _():
                amp_copy(source, s, way, target).wait_recv()
                pl.when(more)(lambda: amp_copy(source, s, way, target).start())
                amp_copy(source, s, 2, sibling).start()

        def pass_row(source, at, away, across_too):
            def one(side, exists, way, target, more):
                origin = source + side * away

                @when(away >= 1, exists)
                def _():
                    int_copy(origin, at, way, target).wait_recv()
                    pl.when(more)(lambda: int_copy(origin, at, way, target).start())
                    if across_too:
                        int_copy(origin, at, 2, across).start()

            one(-1, low_at - away >= 0, 0, right, has_right)
            one(1, low_at + away < wide, 1, left, has_left)

        lower, upper = col - CORES * now, col + CORES * now
        pass_amp(lower, line_at - now >= 0, 0, above, has_above)
        pass_amp(upper, line_at + now < line, 1, below, has_below)
        other = (1 - high_at) * wide + low_at
        for s in range(max(live, pieces)):
            if s < live:
                pass_tile(lower, s, line_at - now >= 0, 0, above, has_above)
                pass_tile(upper, s, line_at + now < line, 1, below, has_below)
            if s < pieces:
                pass_row(pair, s, now, True)

                @when(now == 1)
                def _(s=s):
                    int_copy(other, pieces + s, 2, across).wait_recv()
                    send_row(other, pieces + s)

        for u in range(pieces):
            pass_row(pair, pieces + u, now - 1, False)
            pass_row(other, pieces + u, now - 2, False)
            away = now - 2
            pl.when(away == 0)(lambda u=u: int_copy(other, u, 2, across).wait_recv())
            for side, exists in ((-1, low_at - away >= 0), (1, low_at + away < wide)):
                @when(away >= 1, exists)
                def _(side=side, u=u, away=away):
                    int_copy(other + side * away, u, 2, across).wait_recv()

        def from_sibling(source):
            slot_copy(source, 2, sibling).wait_recv()
            for s in range(live):
                amp_copy(source, s, 2, sibling).wait_recv()

        mate = line_at * CORES + 1 - core
        pl.when(line_at - now >= 0)(lambda: from_sibling(mate - CORES * now))
        when(now >= 1, line_at + now < line)(lambda: from_sibling(mate + CORES * now))

        @pl.loop(0, n_col)
        def _(source):
            @pl.when(amp_slot(source) == now)
            def _():
                for t in range(tiles):
                    place = jnp.broadcast_to(slots[source, pl.ds(t, 1), :], (TILE, TILE))
                    value = jnp.zeros((TILE, TILE), F32)
                    for s in range(live):
                        value = jnp.where(place == s, packed[source, s], value)
                    at = (pl.ds(t // tile_cols * TILE, TILE), pl.ds(t % tile_cols * TILE, TILE))
                    a_high[(source, *at)], a_low[(source, *at)] = split(value)

        @pl.loop(0, n_pair * 2)
        def _(block):
            source, part = block // 2, block % 2

            @pl.when(int_slot(source, part) == now)
            def _():
                span = pl.ds(pl.multiple_of(part * half, half), half)
                value = ints[source, span]
                b_high[source, span], b_low[source, span] = split(value)

        @pl.loop(0, n_col)
        def _(source):
            start = source * depth
            origin, offset = start // int_rows, start % int_rows
            due = jnp.maximum(amp_slot(source), int_slot(origin, offset // half))

            @pl.when(due == now)
            def _():
                span = pl.ds(pl.multiple_of(offset, depth), depth)
                high, low = b_high[origin, span], b_low[origin, span]
                first = a_high[source]
                total = jnp.dot(first, high, preferred_element_type=F32)
                total += jnp.dot(first, low, preferred_element_type=F32)
                total += jnp.dot(a_low[source], high, preferred_element_type=F32)
                out_ref[...] += total

        return 0

    steps = max(line - 1, wide + 1)
    lax.fori_loop(0, steps + 1, step, 0)

    @pl.loop(0, n_col)
    def _(source):
        mine = source % CORES == core
        at = source // CORES

        def drain(way, target):
            slot_copy(source, way, target).wait_send()
            for s in range(live):
                amp_copy(source, s, way, target).wait_send()

        when(mine, at <= line_at, has_above)(lambda: drain(0, above))
        when(mine, at >= line_at, has_below)(lambda: drain(1, below))
        pl.when(mine)(lambda: drain(2, sibling))

    @pl.loop(0, n_pair)
    def _(source):
        same = source // wide == high_at
        at = source % wide

        def drain(first, way, target):
            for u in range(pieces):
                int_copy(source, first + u, way, target).wait_send()

        when(same, at <= low_at, has_right)(lambda: drain(0, 0, right))
        when(same, at >= low_at, has_left)(lambda: drain(0, 1, left))
        pl.when(same)(lambda: drain(0, 2, across))
        when(at <= low_at, has_right)(lambda: drain(pieces, 0, right))
        when(at >= low_at, has_left)(lambda: drain(pieces, 1, left))
        pl.when(source == pair)(lambda: drain(pieces, 2, across))


def local(n_pair, n_col, amplitudes, integrals, amp_tiles, amp_count, int_mask):
    rows, depth = amplitudes.shape
    int_rows, int_cols = integrals.shape
    live = amp_tiles.shape[-1]
    tiles = (rows // TILE) * (depth // TILE)
    half = int_rows // 2
    assert n_pair % 2 == 0 and n_col % CORES == 0
    assert half % depth == 0 and half % TILE == 0
    pieces = int_rows // TILE
    scratch = [
        pltpu.VMEM((rows, depth), F32),
        pltpu.VMEM((n_col, live, TILE, TILE), F32),
        pltpu.VMEM((n_col, tiles, TILE), jnp.int32),
        pltpu.VMEM((n_pair, int_rows, int_cols), F32),
        pltpu.VMEM((n_col, rows, depth), BF16),
        pltpu.VMEM((n_col, rows, depth), BF16),
        pltpu.VMEM((n_pair, int_rows, int_cols), BF16),
        pltpu.VMEM((n_pair, int_rows, int_cols), BF16),
        pltpu.SemaphoreType.DMA,
        pltpu.SemaphoreType.DMA((pieces,)),
        pltpu.SemaphoreType.DMA((n_col, live)),
        pltpu.SemaphoreType.DMA((3, n_col, live)),
        pltpu.SemaphoreType.DMA((n_col,)),
        pltpu.SemaphoreType.DMA((3, n_col)),
        pltpu.SemaphoreType.DMA((n_pair, pieces)),
        pltpu.SemaphoreType.DMA((3, n_pair, pieces)),
    ]
    held = n_col * (live * TILE * TILE * 4 + rows * depth * 4 + 8 * tiles * TILE)
    held += n_pair * int_rows * int_cols * 8 + 3 * rows * (depth + int_cols) * 4
    any_space = pl.BlockSpec(memory_space=pl.ANY)
    scalar = pl.BlockSpec(memory_space=pltpu.SMEM)
    return pl.pallas_call(
        functools.partial(kernel, n_pair, n_col),
        out_shape=jax.ShapeDtypeStruct((rows, int_cols), F32),
        in_specs=[scalar, scalar, scalar, any_space, any_space],
        out_specs=pl.BlockSpec(memory_space=pltpu.VMEM),
        scratch_shapes=scratch,
        compiler_params=pltpu.CompilerParams(
            collective_id=0, has_side_effects=True, vmem_limit_bytes=held + (6 << 20)
        ),
        cost_estimate=pl.CostEstimate(
            flops=6 * rows * depth * n_col * int_cols,
            bytes_accessed=4 * rows * (2 * depth + int_cols),
            transcendentals=0,
        ),
        name="ladder",
    )(amp_tiles.reshape(live), amp_count.reshape(1), int_mask, amplitudes, integrals)


def solution(mesh):
    return jax.shard_map(
        functools.partial(local, mesh.shape["pair"], mesh.shape["col"]),
        mesh=mesh,
        in_specs=(
            P("pair", "col"),
            P("pair", "col"),
            P("pair", "col", None),
            P("pair", "col"),
            P("pair", "col"),
        ),
        out_specs=P("pair", "col"),
        check_vma=False,
    )
```

time: 94.4 us -> 34.9 us (0.37)
  waiting for transfers between devices: 39.1 us -> 0 us
  Pallas kernels: 0 us -> 29.8 us
  between operations: 14.8 us -> 0.67 us
  blocking collectives: 10.7 us -> 0 us
  other arithmetic: 9.29 us -> 0 us
  local copies, waits for them, and re-layouts: 12.2 us -> 4.2 us
  matrix products: 7.93 us -> 0 us
    all_gather x2 -> x0, waiting for transfers between devices: 39.1 us -> none  [the longest x1 21.1 us: local(): lax.all_gather(int_sparse, 'pair', axis=0, tiled=True)]
    pallas_call x0 -> x1, Pallas kernels: none -> 29.8 us  [local(): pl.pallas_call(functools.partial(kernel, n_pair, n_col), out_shape=jax.Sh...]
    all_gather x1 -> x0, blocking collectives: 10.7 us -> none  [local(): lax.all_gather(tile_list, 'col', axis=0, tiled=True)]
    dot_general x1 -> x0, matrix products: 7.93 us -> none  [local(): jnp.dot(panel_whole, lax.all_gather(int_sparse, 'pair', axis=0, tiled=Tru...]
    transpose x2 -> x0, local copies, waits for them, and re-layouts: 6.79 us -> none  [the longest x1 6.75 us: local(): dense_tiles.reshape(tile_rows, col_count * tile_cols, TILE, TILE)]
    scatter-add x1 -> x0, other arithmetic: 6.26 us -> none  [local(): dense_tiles = jnp.zeros((tile_rows * col_count * tile_cols, TILE, TILE),...]
    unnamed x11 -> x10, local copies, waits for them, and re-layouts: 0.74 us -> 4.2 us
    broadcast_in_dim x2 -> x0, local copies, waits for them, and re-layouts: 2.66 us -> none  [the longest x1 2.45 us: local(): jnp.zeros((tile_rows * col_count * tile_cols, TILE, TILE), jnp.float32)]
  transfers between devices with their start and end apart: 2 -> 0, of which waited for: 2 -> 0; matrix products, arithmetic and copies ran while one was open for 19% -> 0% of each run, Pallas kernels for 0% -> 0%
where the time goes in v1:
time: 34.9 us; the launch traced here: 34.7 us
  Pallas kernels  29.8 us (85%)
  local copies, waits for them, and re-layouts  4.2 us (12%)
  between operations  0.67 us (2%)
    pallas_call x1, Pallas kernels, local(): pl.pallas_call(functools.partial(kernel, n_pair, n_col), out_shape=jax.Sh...  29.8 us
    unnamed x10, local copies, waits for them, and re-layouts  4.2 us

profile of v1, /device:TPU:0, one launch (start us, length us, event | category | flops | bytes accessed | tf_op | source)
XLA Modules:
  0.0 34.7 jit_solution(8361492801365906070)
XLA Ops:
  0.7 0.0 copy-start.3
  0.7 0.7 %copy-done.3 = s32[4,2]{0,1:T(2,128)S(1)} copy-done((s32[4,2]{0,1:T(2,128)S(1)}, s32[4,2]{0,1:T(2,128)}, u32[]{:S(2)}) %copy-start.3) | copy-done | bytes 56
  1.3 0.0 copy-start.2
  1.3 0.1 copy.6.mask_ref
  1.4 0.6 %copy-done.2 = s32[1,1,4]{2,1,0:T(1,128)S(1)} copy-done((s32[1,1,4]{2,1,0:T(1,128)S(1)}, s32[1,1,4]{2,1,0:T(1,128)}, u32[]{:S(2)}) %copy-start.2) | copy-done | bytes 40
  2.0 0.0 copy-start
  2.0 1.0 %copy-done = f32[512,256]{1,0:T(8,128)S(1)} copy-done((f32[512,256]{1,0:T(8,128)S(1)}, f32[512,256]{1,0:T(8,128)}, u32[]{:S(2)}) %copy-start) | copy-done | bytes 524312
  3.0 0.0 copy-start.1
  3.0 1.0 %copy-done.1 = f32[512,256]{1,0:T(8,128)S(1)} copy-done((f32[512,256]{1,0:T(8,128)S(1)}, f32[512,256]{1,0:T(8,128)}, u32[]{:S(2)}) %copy-start.1) | copy-done | bytes 524312
  4.1 29.8 %ladder.1 = f32[512,256]{1,0:T(8,128)S(1)} custom-call(s32[4]{0:T(128)S(1)} %bitcast.3, s32[1]{0:T(128)} %bitcast.2.count_ref, s32[4,2]{1,0:T(4,128)S(1)} %copy.6.mask_ref, f32[512,256]{1,0:T(8,128)S(1)} %copy-done, f32[512,256]{1,0:T(8,128)S(1)} %copy-done.1), custom_call_target="tpu_custom_call" | custom-call | flops 1610612736 | bytes 1572864 | tf_op jit(solution)/shard_map/ladder/pallas_call | solution.py:341
  33.9 0.8 %copy.9 = f32[512,256]{1,0:T(8,128)} copy(f32[512,256]{1,0:T(8,128)S(1)} %ladder.1) | data formatting | bytes 1048576
Async XLA Ops:
  0.7 0.7 %copy-start.3 = (s32[4,2]{0,1:T(2,128)S(1)}, s32[4,2]{0,1:T(2,128)}, u32[]{:S(2)}) copy-start(s32[4,2]{0,1:T(2,128)} %param.9) | copy-start | bytes 100
  1.3 0.7 %copy-start.2 = (s32[1,1,4]{2,1,0:T(1,128)S(1)}, s32[1,1,4]{2,1,0:T(1,128)}, u32[]{:S(2)}) copy-start(s32[1,1,4]{2,1,0:T(1,128)} %param.7) | copy-start | bytes 52
  2.0 1.0 %copy-start = (f32[512,256]{1,0:T(8,128)S(1)}, f32[512,256]{1,0:T(8,128)}, u32[]{:S(2)}) copy-start(f32[512,256]{1,0:T(8,128)} %amp_hbm.1) | copy-start | bytes 1572868
  3.0 1.0 %copy-start.1 = (f32[512,256]{1,0:T(8,128)S(1)}, f32[512,256]{1,0:T(8,128)}, u32[]{:S(2)}) copy-start(f32[512,256]{1,0:T(8,128)} %int_hbm.1) | copy-start | bytes 1572868

commit v2 on v1

--- a/solution.py
+++ b/solution.py
@@ -9,6 +9,7 @@
 
 TILE = 128
 CORES = 2
+VMEM_BYTES = 60 << 20
 MESH = pl.DeviceIdType.MESH
 BF16 = jnp.bfloat16
 F32 = jnp.float32
@@ -27,9 +28,9 @@
 
 
 def kernel(
-    n_pair, n_col, list_ref, count_ref, mask_ref, amp_hbm, int_hbm, out_ref,
-    amp, packed, slots, ints, a_high, a_low, b_high, b_low,
-    load_amp, load_int, amp_recv, amp_send, slot_recv, slot_send, int_recv, int_send,
+    n_pair, n_col, list_hbm, count_hbm, mask_hbm, amp_hbm, int_hbm, out_ref,
+    list_ref, count_ref, mask_ref, amp, packed, slots, ints, a_high, a_low, b_high, b_low,
+    load_small, load_amp, load_int, amp_recv, amp_send, slot_recv, slot_send, int_recv, int_send,
 ):
     live = packed.shape[1]
     rows, depth = amp.shape
@@ -60,7 +61,15 @@
         )
         for at in range(2 * pieces)
     ]
+    small_loads = [
+        pltpu.make_async_copy(source, target, load_small.at[at])
+        for at, (source, target) in enumerate(
+            ((list_hbm, list_ref), (count_hbm, count_ref), (mask_hbm, mask_ref))
+        )
+    ]
     amp_load = pltpu.make_async_copy(amp_hbm, amp, load_amp)
+    for load in small_loads:
+        load.start()
     amp_load.start()
     for load in int_loads:
         load.start()
@@ -77,11 +86,6 @@
             greet()
         else:
             pl.when(exists)(greet)
-    peers = 2
-    for _, exists in partners[2:]:
-        peers += jnp.where(exists, 1, 0)
-    pl.semaphore_wait(barrier, peers)
-
     def amp_copy(source, slot, way, target):
         ref = packed.at[source, slot]
         return pltpu.make_async_remote_copy(
@@ -106,11 +110,13 @@
             device_id=target, device_id_type=MESH,
         )
 
-    amp_load.wait()
+    out_ref[...] = jnp.zeros_like(out_ref)
+    for load in small_loads:
+        load.wait()
     numbers = [
         jnp.where(
-            jnp.full((1, TILE), count_ref[0], jnp.int32) > s,
-            jnp.full((1, TILE), list_ref[s], jnp.int32),
+            jnp.full((1, TILE), count_ref[0, 0], jnp.int32) > s,
+            jnp.full((1, TILE), list_ref[0, 0, s], jnp.int32),
             -1,
         )
         for s in range(live)
@@ -120,13 +126,7 @@
         for s in range(live):
             place = jnp.where(numbers[s] == t, s, place)
         slots[col, pl.ds(t, 1), :] = place
-
-    def send_own_amp(copy):
-        pl.when(has_above)(lambda: copy(0, above).start())
-        pl.when(has_below)(lambda: copy(1, below).start())
-        copy(2, sibling).start()
-
-    send_own_amp(lambda way, target: slot_copy(col, way, target))
+    amp_load.wait()
     for s in range(live):
         number = jnp.broadcast_to(numbers[s], (TILE, TILE))
         value = jnp.zeros((TILE, TILE), F32)
@@ -134,30 +134,39 @@
             at = (pl.ds(t // tile_cols * TILE, TILE), pl.ds(t % tile_cols * TILE, TILE))
             value = jnp.where(number == t, amp[at], value)
         packed[col, s] = value
-        send_own_amp(lambda way, target, s=s: amp_copy(col, s, way, target))
-
-    def ready(at):
+
+    for at in range(2 * pieces):
         int_loads[at].wait()
         span = pl.ds(at * piece, piece)
         for c in range(int_cols // TILE):
-            keep = mask_ref[at * piece // TILE, c].astype(F32)
+            keep = mask_ref[c, at * piece // TILE].astype(F32)
             cols = pl.ds(c * TILE, TILE)
             ints[pair, span, cols] = ints[pair, span, cols] * keep
+
+    peers = 2
+    for _, exists in partners[2:]:
+        peers += jnp.where(exists, 1, 0)
+    pl.semaphore_wait(barrier, peers)
+
+    def send_own_amp(copy):
+        pl.when(has_above)(lambda: copy(0, above).start())
+        pl.when(has_below)(lambda: copy(1, below).start())
+        copy(2, sibling).start()
 
     def send_row(source, at):
         pl.when(has_right)(lambda: int_copy(source, at, 0, right).start())
         pl.when(has_left)(lambda: int_copy(source, at, 1, left).start())
 
-    for u in range(pieces):
-        ready(u)
-        send_row(pair, u)
-        ready(pieces + u)
-        int_copy(pair, pieces + u, 2, across).start()
+    send_own_amp(lambda way, target: slot_copy(col, way, target))
+    for s in range(max(live, pieces)):
+        if s < live:
+            send_own_amp(lambda way, target, s=s: amp_copy(col, s, way, target))
+        if s < pieces:
+            send_row(pair, s)
+            int_copy(pair, pieces + s, 2, across).start()
     for u in range(pieces):
         send_row(pair, pieces + u)
         int_copy(pair, u, 2, across).start()
-
-    out_ref[...] = jnp.zeros_like(out_ref)
 
     def amp_slot(source):
         return jnp.abs(source // CORES - line_at)
@@ -229,22 +238,6 @@
             for s in range(live):
                 amp_copy(source, s, 2, sibling).wait_recv()
 
-        mate = line_at * CORES + 1 - core
-        pl.when(line_at - now >= 0)(lambda: from_sibling(mate - CORES * now))
-        when(now >= 1, line_at + now < line)(lambda: from_sibling(mate + CORES * now))
-
-        @pl.loop(0, n_col)
-        def _(source):
-            @pl.when(amp_slot(source) == now)
-            def _():
-                for t in range(tiles):
-                    place = jnp.broadcast_to(slots[source, pl.ds(t, 1), :], (TILE, TILE))
-                    value = jnp.zeros((TILE, TILE), F32)
-                    for s in range(live):
-                        value = jnp.where(place == s, packed[source, s], value)
-                    at = (pl.ds(t // tile_cols * TILE, TILE), pl.ds(t % tile_cols * TILE, TILE))
-                    a_high[(source, *at)], a_low[(source, *at)] = split(value)
-
         @pl.loop(0, n_pair * 2)
         def _(block):
             source, part = block // 2, block % 2
@@ -255,21 +248,45 @@
                 value = ints[source, span]
                 b_high[source, span], b_low[source, span] = split(value)
 
-        @pl.loop(0, n_col)
-        def _(source):
-            start = source * depth
-            origin, offset = start // int_rows, start % int_rows
-            due = jnp.maximum(amp_slot(source), int_slot(origin, offset // half))
-
-            @pl.when(due == now)
+        mate = line_at * CORES + 1 - core
+
+        @pl.loop(0, CORES)
+        def _(turn):
+            @pl.when(turn == 1)
             def _():
-                span = pl.ds(pl.multiple_of(offset, depth), depth)
-                high, low = b_high[origin, span], b_low[origin, span]
-                first = a_high[source]
-                total = jnp.dot(first, high, preferred_element_type=F32)
-                total += jnp.dot(first, low, preferred_element_type=F32)
-                total += jnp.dot(a_low[source], high, preferred_element_type=F32)
-                out_ref[...] += total
+                pl.when(line_at - now >= 0)(lambda: from_sibling(mate - CORES * now))
+                when(now >= 1, line_at + now < line)(lambda: from_sibling(mate + CORES * now))
+
+            @pl.loop(0, line)
+            def _(place_at):
+                source = place_at * CORES + (core + turn) % CORES
+
+                @pl.when(amp_slot(source) == now)
+                def _():
+                    for t in range(tiles):
+                        place = jnp.broadcast_to(slots[source, pl.ds(t, 1), :], (TILE, TILE))
+                        value = jnp.zeros((TILE, TILE), F32)
+                        for s in range(live):
+                            value = jnp.where(place == s, packed[source, s], value)
+                        at = (
+                            pl.ds(t // tile_cols * TILE, TILE),
+                            pl.ds(t % tile_cols * TILE, TILE),
+                        )
+                        a_high[(source, *at)], a_low[(source, *at)] = split(value)
+
+                start = source * depth
+                origin, offset = start // int_rows, start % int_rows
+                due = jnp.maximum(amp_slot(source), int_slot(origin, offset // half))
+
+                @pl.when(due == now)
+                def _():
+                    span = pl.ds(pl.multiple_of(offset, depth), depth)
+                    high, low = b_high[origin, span], b_low[origin, span]
+                    first = a_high[source]
+                    total = jnp.dot(first, high, preferred_element_type=F32)
+                    total += jnp.dot(first, low, preferred_element_type=F32)
+                    total += jnp.dot(a_low[source], high, preferred_element_type=F32)
+                    out_ref[...] += total
 
         return 0
 
@@ -317,6 +334,9 @@
     assert half % depth == 0 and half % TILE == 0
     pieces = int_rows // TILE
     scratch = [
+        pltpu.SMEM(amp_tiles.shape, jnp.int32),
+        pltpu.SMEM(amp_count.shape, jnp.int32),
+        pltpu.SMEM(int_mask.shape[::-1], jnp.int32),
         pltpu.VMEM((rows, depth), F32),
         pltpu.VMEM((n_col, live, TILE, TILE), F32),
         pltpu.VMEM((n_col, tiles, TILE), jnp.int32),
@@ -325,6 +345,7 @@
         pltpu.VMEM((n_col, rows, depth), BF16),
         pltpu.VMEM((n_pair, int_rows, int_cols), BF16),
         pltpu.VMEM((n_pair, int_rows, int_cols), BF16),
+        pltpu.SemaphoreType.DMA((3,)),
         pltpu.SemaphoreType.DMA,
         pltpu.SemaphoreType.DMA((pieces,)),
         pltpu.SemaphoreType.DMA((n_col, live)),
@@ -334,18 +355,14 @@
         pltpu.SemaphoreType.DMA((n_pair, pieces)),
         pltpu.SemaphoreType.DMA((3, n_pair, pieces)),
     ]
-    held = n_col * (live * TILE * TILE * 4 + rows * depth * 4 + 8 * tiles * TILE)
-    held += n_pair * int_rows * int_cols * 8 + 3 * rows * (depth + int_cols) * 4
-    any_space = pl.BlockSpec(memory_space=pl.ANY)
-    scalar = pl.BlockSpec(memory_space=pltpu.SMEM)
     return pl.pallas_call(
         functools.partial(kernel, n_pair, n_col),
         out_shape=jax.ShapeDtypeStruct((rows, int_cols), F32),
-        in_specs=[scalar, scalar, scalar, any_space, any_space],
+        in_specs=[pl.BlockSpec(memory_space=pltpu.HBM)] * 5,
         out_specs=pl.BlockSpec(memory_space=pltpu.VMEM),
         scratch_shapes=scratch,
         compiler_params=pltpu.CompilerParams(
-            collective_id=0, has_side_effects=True, vmem_limit_bytes=held + (6 << 20)
+            collective_id=0, has_side_effects=True, vmem_limit_bytes=VMEM_BYTES
         ),
         cost_estimate=pl.CostEstimate(
             flops=6 * rows * depth * n_col * int_cols,
@@ -353,7 +370,7 @@
             transcendentals=0,
         ),
         name="ladder",
-    )(amp_tiles.reshape(live), amp_count.reshape(1), int_mask, amplitudes, integrals)
+    )(amp_tiles, amp_count, int_mask.T, amplitudes, integrals)
 
 
 def solution(mesh):

time: 34.9 us -> 30.3 us (0.87)
  local copies, waits for them, and re-layouts: 4.2 us -> 1.87 us
  Pallas kernels: 29.8 us -> 27.6 us
    unnamed x10 -> x1, local copies, waits for them, and re-layouts: 4.2 us -> 1.87 us
    pallas_call x1, Pallas kernels: 29.8 us -> 27.6 us  [local(): pl.pallas_call(functools.partial(kernel, n_pair, n_col), out_shape=jax.Sh...]
where the time goes in v2:
time: 30.3 us; the launch traced here: 30.2 us
  Pallas kernels  27.6 us (91%)
  local copies, waits for them, and re-layouts  1.87 us (6%)
  between operations  0.66 us (2%)
    pallas_call x1, Pallas kernels, local(): pl.pallas_call(functools.partial(kernel, n_pair, n_col), out_shape=jax.Sh...  27.6 us
    unnamed x1, local copies, waits for them, and re-layouts  1.87 us

profile of v2, /device:TPU:0, one launch (start us, length us, event | category | flops | bytes accessed | tf_op | source)
XLA Modules:
  0.0 30.2 jit_solution(11076252140907634933)
XLA Ops:
  0.7 27.6 %ladder.1 = f32[512,256]{1,0:T(8,128)} custom-call(s32[1,1,4]{2,1,0:T(1,128)} %list_hbm.1, s32[1,1]{1,0:T(1,128)S(6)} %copy.7.count_hbm, s32[2,4]{1,0:T(2,128)} %bitcast.1, f32[512,256]{1,0:T(8,128)} %amp_hbm.1, f32[512,256]{1,0:T(8,128)} %int_hbm.1), custom_call_target="tpu_custom_call" | custom-call | flops 1610612736 | bytes 1572864 | tf_op jit(solution)/shard_map/ladder/pallas_call | solution.py:358
  28.3 1.9 %copy.8 = f32[512,256]{1,0:T(8,128)} copy(f32[512,256]{1,0:T(8,128)} %ladder.1) | data formatting | bytes 1048576

commit v3 on v2

--- a/solution.py
+++ b/solution.py
@@ -21,10 +21,12 @@
 
 
 def when(*conditions):
-    together = conditions[0]
-    for condition in conditions[1:]:
-        together = jnp.logical_and(together, condition)
-    return pl.when(together)
+    if any(condition is False for condition in conditions):
+        return lambda body: None
+    traced = [condition for condition in conditions if condition is not True]
+    if not traced:
+        return lambda body: body()
+    return pl.when(functools.reduce(jnp.logical_and, traced))
 
 
 def kernel(
@@ -52,6 +54,10 @@
     right, left = {"pair": pair + 1}, {"pair": pair - 1}
     has_above, has_below = line_at < line - 1, line_at > 0
     has_right, has_left = low_at < wide - 1, low_at > 0
+    far = {"col": (line - 1 - line_at) * CORES + core}
+    is_end = (line_at == 0) | (line_at == line - 1) if line > 2 else False
+    passes_up = (line_at < line - 2) if line > 2 else has_above
+    passes_down = (line_at > 1) if line > 2 else has_below
 
     int_loads = [
         pltpu.make_async_copy(
@@ -77,15 +83,12 @@
     barrier = pltpu.get_barrier_semaphore()
     partners = (
         (sibling, None), (across, None), (above, has_above), (below, has_below),
-        (right, has_right), (left, has_left),
+        (right, has_right), (left, has_left), (far, is_end),
     )
     for partner, exists in partners:
         def greet(partner=partner):
             pl.semaphore_signal(barrier, inc=1, device_id=partner, device_id_type=MESH)
-        if exists is None:
-            greet()
-        else:
-            pl.when(exists)(greet)
+        when(exists is None or exists)(greet)
     def amp_copy(source, slot, way, target):
         ref = packed.at[source, slot]
         return pltpu.make_async_remote_copy(
@@ -145,12 +148,14 @@
 
     peers = 2
     for _, exists in partners[2:]:
-        peers += jnp.where(exists, 1, 0)
+        if exists is not False:
+            peers += jnp.where(exists, 1, 0)
     pl.semaphore_wait(barrier, peers)
 
     def send_own_amp(copy):
         pl.when(has_above)(lambda: copy(0, above).start())
         pl.when(has_below)(lambda: copy(1, below).start())
+        when(is_end)(lambda: copy(3, far).start())
         copy(2, sibling).start()
 
     def send_row(source, at):
@@ -178,26 +183,26 @@
         far = jnp.where(part == 0, away + 2, jnp.where(away > 0, away + 2, 1))
         return jnp.where(same, near, far)
 
-    def step(now, _):
+    def step(now):
         def pass_amp(source, exists, way, target, more):
-            @when(now >= 1, exists)
+            @when(now >= 1, now < line, exists)
             def _():
                 slot_copy(source, way, target).wait_recv()
-                pl.when(more)(lambda: slot_copy(source, way, target).start())
+                when(more)(lambda: slot_copy(source, way, target).start())
                 slot_copy(source, 2, sibling).start()
 
         def pass_tile(source, s, exists, way, target, more):
-            @when(now >= 1, exists)
+            @when(now >= 1, now < line, exists)
             def _():
                 amp_copy(source, s, way, target).wait_recv()
-                pl.when(more)(lambda: amp_copy(source, s, way, target).start())
+                when(more)(lambda: amp_copy(source, s, way, target).start())
                 amp_copy(source, s, 2, sibling).start()
 
         def pass_row(source, at, away, across_too):
             def one(side, exists, way, target, more):
                 origin = source + side * away
 
-                @when(away >= 1, exists)
+                @when(away >= 1, away < wide, exists)
                 def _():
                     int_copy(origin, at, way, target).wait_recv()
                     pl.when(more)(lambda: int_copy(origin, at, way, target).start())
@@ -208,13 +213,17 @@
             one(1, low_at + away < wide, 1, left, has_left)
 
         lower, upper = col - CORES * now, col + CORES * now
-        pass_amp(lower, line_at - now >= 0, 0, above, has_above)
-        pass_amp(upper, line_at + now < line, 1, below, has_below)
+        more_above = has_above if line == 2 else has_above & ((line_at != now) | passes_up)
+        more_below = has_below if line == 2 else has_below & (
+            (line_at + now != line - 1) | passes_down
+        )
+        pass_amp(lower, line_at - now >= 0, 0, above, more_above)
+        pass_amp(upper, line_at + now < line, 1, below, more_below)
         other = (1 - high_at) * wide + low_at
         for s in range(max(live, pieces)):
             if s < live:
-                pass_tile(lower, s, line_at - now >= 0, 0, above, has_above)
-                pass_tile(upper, s, line_at + now < line, 1, below, has_below)
+                pass_tile(lower, s, line_at - now >= 0, 0, above, more_above)
+                pass_tile(upper, s, line_at + now < line, 1, below, more_below)
             if s < pieces:
                 pass_row(pair, s, now, True)
 
@@ -227,9 +236,9 @@
             pass_row(pair, pieces + u, now - 1, False)
             pass_row(other, pieces + u, now - 2, False)
             away = now - 2
-            pl.when(away == 0)(lambda u=u: int_copy(other, u, 2, across).wait_recv())
+            when(away == 0)(lambda u=u: int_copy(other, u, 2, across).wait_recv())
             for side, exists in ((-1, low_at - away >= 0), (1, low_at + away < wide)):
-                @when(away >= 1, exists)
+                @when(away >= 1, away < wide, exists)
                 def _(side=side, u=u, away=away):
                     int_copy(other + side * away, u, 2, across).wait_recv()
 
@@ -254,8 +263,8 @@
         def _(turn):
             @pl.when(turn == 1)
             def _():
-                pl.when(line_at - now >= 0)(lambda: from_sibling(mate - CORES * now))
-                when(now >= 1, line_at + now < line)(lambda: from_sibling(mate + CORES * now))
+                when(line_at - now >= 0)(lambda: from_sibling(mate - CORES * now))
+                when(now >= 1, now < line, line_at + now < line)(lambda: from_sibling(mate + CORES * now))
 
             @pl.loop(0, line)
             def _(place_at):
@@ -288,10 +297,8 @@
                     total += jnp.dot(a_low[source], high, preferred_element_type=F32)
                     out_ref[...] += total
 
-        return 0
-
-    steps = max(line - 1, wide + 1)
-    lax.fori_loop(0, steps + 1, step, 0)
+    for now in range(max(line - 1, wide + 1) + 1):
+        step(now)
 
     @pl.loop(0, n_col)
     def _(source):
@@ -303,8 +310,13 @@
             for s in range(live):
                 amp_copy(source, s, way, target).wait_send()
 
-        when(mine, at <= line_at, has_above)(lambda: drain(0, above))
-        when(mine, at >= line_at, has_below)(lambda: drain(1, below))
+        up, down = at <= line_at, at >= line_at
+        if line > 2:
+            up &= (at > 0) | (line_at != line - 2)
+            down &= (at < line - 1) | (line_at != 1)
+        when(mine, up, has_above)(lambda: drain(0, above))
+        when(mine, down, has_below)(lambda: drain(1, below))
+        when(mine, at == line_at, is_end)(lambda: drain(3, far))
         pl.when(mine)(lambda: drain(2, sibling))
 
     @pl.loop(0, n_pair)
@@ -349,15 +361,15 @@
         pltpu.SemaphoreType.DMA,
         pltpu.SemaphoreType.DMA((pieces,)),
         pltpu.SemaphoreType.DMA((n_col, live)),
-        pltpu.SemaphoreType.DMA((3, n_col, live)),
+        pltpu.SemaphoreType.DMA((4, n_col, live)),
         pltpu.SemaphoreType.DMA((n_col,)),
-        pltpu.SemaphoreType.DMA((3, n_col)),
+        pltpu.SemaphoreType.DMA((4, n_col)),
         pltpu.SemaphoreType.DMA((n_pair, pieces)),
         pltpu.SemaphoreType.DMA((3, n_pair, pieces)),
     ]
     return pl.pallas_call(
         functools.partial(kernel, n_pair, n_col),
-        out_shape=jax.ShapeDtypeStruct((rows, int_cols), F32),
+        out_shape=pltpu.VMEM((rows, int_cols), F32),
         in_specs=[pl.BlockSpec(memory_space=pltpu.HBM)] * 5,
         out_specs=pl.BlockSpec(memory_space=pltpu.VMEM),
         scratch_shapes=scratch,

time: 30.3 us -> 31 us (1.023)
  Pallas kernels: 27.6 us -> 29.4 us
  local copies, waits for them, and re-layouts: 1.87 us -> 0.8 us
    pallas_call x1, Pallas kernels: 27.6 us -> 29.4 us  [local(): pl.pallas_call(functools.partial(kernel, n_pair, n_col), out_shape=pltpu....]
    unnamed x1, local copies, waits for them, and re-layouts: 1.87 us -> 0.8 us
where the time goes in v3:
time: 31 us; the launch traced here: 30.8 us
  Pallas kernels  29.4 us (95%)
  local copies, waits for them, and re-layouts  0.8 us (3%)
  between operations  0.66 us (2%)
    pallas_call x1, Pallas kernels, local(): pl.pallas_call(functools.partial(kernel, n_pair, n_col), out_shape=pltpu....  29.4 us
    unnamed x1, local copies, waits for them, and re-layouts  0.8 us

profile of v3, /device:TPU:0, one launch (start us, length us, event | category | flops | bytes accessed | tf_op | source)
XLA Modules:
  0.0 30.8 jit_solution(9866209848554999533)
XLA Ops:
  0.7 29.4 %ladder.1 = f32[512,256]{1,0:T(8,128)S(1)} custom-call(s32[1,1,4]{2,1,0:T(1,128)} %list_hbm.1, s32[1,1]{1,0:T(1,128)S(6)} %copy.8.count_hbm, s32[2,4]{1,0:T(2,128)} %bitcast.1, f32[512,256]{1,0:T(8,128)} %amp_hbm.1, f32[512,256]{1,0:T(8,128)} %int_hbm.1), custom_call_target="tpu_custom_call" | custom-call | flops 1610612736 | bytes 1572864 | tf_op jit(solution)/shard_map/ladder/pallas_call | solution.py:370
  30.0 0.8 %copy.7 = f32[512,256]{1,0:T(8,128)} copy(f32[512,256]{1,0:T(8,128)S(1)} %ladder.1) | data formatting | bytes 1048576
